TPU v7x, 256 devices: a whole 4x4x8 slice. The times are simulated.
256 devices in a mesh: vert: 128 (over z, y, x), qcol: 2 (over core).
Axes of the slice: x: 4, y: 4, z: 8, core: 2. Of those that a mesh axis runs over, the one named last changes fastest.
Arguments:
- descriptors: bfloat16 [262144, 2048], P('vert'), may hold values from -0.8984375 to 0.8984375
- queries: bfloat16 [512, 2048], P('qcol', 'vert'), may hold values from -0.8984375 to 0.8984375
- tiles: bfloat16 [6144, 128, 128], P('vert'), may hold values from 0 to 1, as said below
- tile_cols: int32 [128, 3, 16], replicated, may hold values from 0 to 15, as said below
- part_size: int32 [128], replicated, may hold values from 1024 to 2048, as said below
Outputs:
- ranking: float32 [262144, 512], P('vert', 'qcol')
- residual: float32 [262144, 512], P('vert', 'qcol')
Inputs may be any that keep to these rules, and one draw needn't show every extreme that they name: For each part d and slot j, tile_cols[d, j, :] is a permutation of 0 to 15. `part_size`: some part has exactly 2048 live vertices and some exactly 1024. tiles are sparse and nonnegative; every row and every column of B sums to at most 1.01.
All inputs are finite; a program needn't handle non-finite values.
Results may differ from a plain program's by a relative error of at most 0.0003.
Values may be sent and summed in bfloat16 or wider, within the bound.
A program may use at most 128 MiB of HBM per device.

v0:
```python
import jax
import jax.numpy as jnp
from jax import lax
from jax.sharding import PartitionSpec as P

ITERS = 2


def padded(block, sides, width):
    for axis, dim in sides:
        count = lax.axis_size(axis)
        forward = [(i, i + 1) for i in range(count - 1)]
        forward.append((count - 1, 0))
        backward = [(target, source) for source, target in forward]
        low = lax.ppermute(
            lax.slice_in_dim(block, block.shape[dim] - width, None, axis=dim), axis, forward
        )
        high = lax.ppermute(lax.slice_in_dim(block, 0, width, axis=dim), axis, backward)
        block = jnp.concatenate([low, block, high], axis=dim)
    return block


def shifted(x, axis, by):
    peers = lax.axis_size(axis)
    return lax.ppermute(x, axis, [(i, (i + by) % peers) for i in range(peers)])


def transposed(blocks_slot, rows3, cols_row):
    moved = jnp.einsum("rba,rbq->raq", blocks_slot, rows3, precision=lax.Precision.HIGHEST)
    return moved[jnp.argsort(cols_row)]


def body(descriptors, queries, tiles, tile_cols, part_size):
    rows = descriptors.shape[0]
    qdev = queries.shape[0]
    tile = tiles.shape[1]
    rtiles = rows // tile
    slots = tiles.shape[0] // rtiles
    here = lax.axis_index("vert")
    sims = lax.dot_general(
        descriptors,
        lax.all_gather(queries, "vert", axis=1, tiled=True),
        (((1,), (1,)), ((), ())),
        preferred_element_type=jnp.float32,
    )
    live_count = lax.dynamic_index_in_dim(part_size, here, 0, keepdims=False)
    live = (lax.iota(jnp.int32, rows) < live_count).astype(jnp.float32)[:, None]
    seeds = live * jnp.maximum(sims, 0.0) ** 3
    blocks = tiles.astype(jnp.float32).reshape(slots, rtiles, tile, tile)
    own_cols = lax.dynamic_index_in_dim(tile_cols, here, 0, keepdims=False)

    def squares(values):
        return lax.psum(jnp.sum(values * values, axis=0), "vert")

    ranking = jnp.zeros_like(seeds)
    residual = seeds
    direction = seeds
    norm_now = squares(residual)
    for step in range(ITERS):
        widened = padded(direction, (("vert", 0),), rows)
        forward = jnp.zeros((rtiles, tile, qdev), jnp.float32)
        for slot in range(slots):
            source = widened[slot * rows : (slot + 1) * rows].reshape(rtiles, tile, qdev)
            picked = source[own_cols[slot]]
            forward = forward + jnp.einsum(
                "rab,rbq->raq", blocks[slot], picked, precision=lax.Precision.HIGHEST
            )
        own3 = direction.reshape(rtiles, tile, qdev)
        middle = transposed(blocks[1], own3, own_cols[1])
        toward_low = transposed(blocks[0], own3, own_cols[0])
        toward_high = transposed(blocks[slots - 1], own3, own_cols[slots - 1])
        back = middle + shifted(toward_low, "vert", -1) + shifted(toward_high, "vert", 1)
        both = (forward + back).reshape(rows, qdev)
        image = direction - 0.99 * live * (0.5 * both)
        curve = lax.psum(jnp.sum(direction * image, axis=0), "vert")
        alpha = norm_now / curve
        ranking = ranking + alpha[None, :] * direction
        residual = residual - alpha[None, :] * image
        norm_next = squares(residual)
        direction = residual + (norm_next / norm_now)[None, :] * direction
        norm_now = norm_next
    return (ranking, residual)


def solution(mesh):
    placed = (P("vert", None), P("qcol", "vert"), P("vert", None, None), P(), P())
    return jax.shard_map(
        body,
        mesh=mesh,
        in_specs=placed,
        out_specs=(P("vert", "qcol"), P("vert", "qcol")),
        check_vma=False,
    )
```

profile of v0, /device:TPU:0, one launch (start us, length us, event | category | flops | bytes accessed | tf_op | source)
XLA Modules:
  0.0 1348.9 jit_solution(10652084589290533953)
XLA Ops:
  14.6 100.5 %all-gather.2.cloned.1.call-done = bf16[256,2048]{0,1:T(8,128)(2,1)} async-done(((bf16[256,16]{0,1:T(8,128)(2,1)}), bf16[256,2048]{0,1:T(8,128)(2,1)}) %all-gather.2.cloned.1.call-update) | async-done | bytes 1048592 | tf_op jit(solution)/shard_map/all_gather | solution.py:42
  115.1 6.1 fusion
  122.6 6.1 collective-permute-start.1
  128.7 4.3 convolution_bitcast_fusion.4
  140.9 4.3 convolution_bitcast_fusion.3
  153.1 4.3 convolution_bitcast_fusion.5
  165.9 4.1 fusion.17
  170.0 5.3 collective-permute-done
  175.4 3.6 gather_fusion
  179.0 3.7 gather_fusion.2
  185.7 28.8 %collective-permute-done.2 = f32[16,128,256]{2,1,0:T(8,128)} collective-permute-done((f32[16,128,256]{2,1,0:T(8,128)}, f32[16,128,256]{2,1,0:T(8,128)}, u32[]{:S(2)}, u32[]{:S(2)}) %collective-permute-start.2) | collective-permute-done | bytes 2097184 | tf_op jit(solution)/shard_map/ppermute | solution.py:25
  215.2 5.1 bitcast_add_fusion.1
  221.7 349.4 %all-reduce = (f32[256]{0:T(256)S(1)}, f32[256]{0:T(256)S(1)}) all-reduce(f32[256]{0:T(256)S(1)} %get-tuple-element.9, f32[256]{0:T(256)S(1)} %get-tuple-element.8), channel_id=1, replica_groups=mesh['vert'=128,'qcol'=2] {'vert'}, use_global_device_ids=true, to_apply=%region_1.2 | all-reduce | flops 512 | bytes 4096 | tf_op jit(solution)/shard_map/psum | solution.py:53
  573.1 343.0 %psum.30 = f32[256]{0:T(256)S(1)} all-reduce(f32[256]{0:T(256)S(1)} %multiply_reduce_fusion.1), channel_id=1, replica_groups=mesh['vert'=128,'qcol'=2] {'vert'}, use_global_device_ids=true, to_apply=%region_8.9 | all-reduce | flops 256 | bytes 2048 | tf_op jit(solution)/shard_map/psum | solution.py:53
  921.5 5.5 collective-permute-start.5
  927.0 4.9 convolution_bitcast_fusion.1
  938.4 5.0 convolution_bitcast_fusion
  955.6 5.0 convolution_bitcast_fusion.2
  963.5 3.6 gather_fusion.9
  967.1 4.1 fusion.14
  971.3 3.6 gather_fusion.6
  981.9 5.1 bitcast_add_fusion
  990.3 347.1 %psum.31 = f32[256]{0:T(256)S(1)} all-reduce(f32[256]{0:T(256)S(1)} %multiply_reduce_fusion), channel_id=1, replica_groups=mesh['vert'=128,'qcol'=2] {'vert'}, use_global_device_ids=true, to_apply=%region_10.11 | all-reduce | flops 256 | bytes 2048 | tf_op jit(solution)/shard_map/psum | solution.py:75
  1337.5 4.6 multiply_subtract_fusion
  (70 shorter events, 77.5 us)
Async XLA Ops:
  7.2 107.9 %all-gather.2.cloned.1.call-start = ((), (), s32[]{:S(2)}) async-start(), calls=%async_computation | async-start | bytes 1056768 | tf_op jit(solution)/shard_map/all_gather | solution.py:42
  121.2 54.2 %collective-permute-start = (f32[2048,256]{1,0:T(8,128)S(1)}, f32[2048,256]{1,0:T(8,128)}, u32[]{:S(2)}, u32[]{:S(2)}) collective-permute-start(f32[2048,256]{1,0:T(8,128)S(1)} %fusion), channel_id=1, source_target_pairs={{0,2},{2,4},{4,6},{6,8},{8,10},{10,12},{12,14},{14,16},{16,18},{18... | collective-permute-start | bytes 6291464 | tf_op jit(solution)/shard_map/ppermute | solution.py:15
  122.6 56.4 %collective-permute-start.1 = (f32[2048,256]{1,0:T(8,128)S(1)}, f32[2048,256]{1,0:T(8,128)}, u32[]{:S(2)}, u32[]{:S(2)}) collective-permute-start(f32[2048,256]{1,0:T(8,128)S(1)} %fusion), channel_id=1, source_target_pairs={{2,0},{4,2},{6,4},{8,6},{10,8},{12,10},{14,12},{16,14},{18,16},{20... | collective-permute-start | bytes 6291464 | tf_op jit(solution)/shard_map/ppermute | solution.py:18
  139.5 74.9 %collective-permute-start.2 = (f32[16,128,256]{2,1,0:T(8,128)}, f32[16,128,256]{2,1,0:T(8,128)}, u32[]{:S(2)}, u32[]{:S(2)}) collective-permute-start(f32[16,128,256]{2,1,0:T(8,128)} %gather_fusion.4), channel_id=1, source_target_pairs={{0,254},{2,0},{4,2},{6,4},{8,6},{10,8},{12,10},{14,12},{16,14},{18... | collective-permute-start | bytes 6291464 | tf_op jit(solution)/shard_map/ppermute | solution.py:25
  151.6 63.5 %collective-permute-start.3 = (f32[16,128,256]{2,1,0:T(8,128)}, f32[16,128,256]{2,1,0:T(8,128)}, u32[]{:S(2)}, u32[]{:S(2)}) collective-permute-start(f32[16,128,256]{2,1,0:T(8,128)} %gather_fusion.5), channel_id=1, source_target_pairs={{0,2},{2,4},{4,6},{6,8},{8,10},{10,12},{12,14},{14,16},{16,18},{18... | collective-permute-start | bytes 6291464 | tf_op jit(solution)/shard_map/ppermute | solution.py:25
  182.7 32.5 %copy-start.4 = (f32[16,128,256]{2,1,0:T(8,128)S(1)}, f32[16,128,256]{2,1,0:T(8,128)}, u32[]{:S(2)}) copy-start(f32[16,128,256]{2,1,0:T(8,128)} %gather_fusion.3) | copy-start | bytes 6291460
  182.7 32.5 %copy-start.5 = (f32[16,256,128]{1,2,0:T(8,128)S(1)}, f32[16,256,128]{1,2,0:T(8,128)}, u32[]{:S(2)}) copy-start(f32[16,256,128]{1,2,0:T(8,128)} %fusion.17) | copy-start | bytes 6291460
  220.3 1.4 copy-start
  919.5 51.7 %collective-permute-start.4 = (f32[2048,256]{1,0:T(8,128)}, f32[2048,256]{1,0:T(8,128)}, u32[]{:S(2)}, u32[]{:S(2)}) collective-permute-start(f32[2048,256]{1,0:T(8,128)} %multiply_add_fusion.1), channel_id=1, source_target_pairs={{0,2},{2,4},{4,6},{6,8},{8,10},{10,12},{12,14},{14,16},{16,18},{18... | collective-permute-start | bytes 6291464 | tf_op jit(solution)/shard_map/ppermute | solution.py:15
  921.5 53.4 %collective-permute-start.5 = (f32[2048,256]{1,0:T(8,128)}, f32[2048,256]{1,0:T(8,128)}, u32[]{:S(2)}, u32[]{:S(2)}) collective-permute-start(f32[2048,256]{1,0:T(8,128)} %multiply_add_fusion.1), channel_id=1, source_target_pairs={{2,0},{4,2},{6,4},{8,6},{10,8},{12,10},{14,12},{16,14},{18,16},{20... | collective-permute-start | bytes 6291464 | tf_op jit(solution)/shard_map/ppermute | solution.py:18
  938.4 43.0 %collective-permute-start.6 = (f32[16,128,256]{2,1,0:T(8,128)}, f32[16,128,256]{2,1,0:T(8,128)}, u32[]{:S(2)}, u32[]{:S(2)}) collective-permute-start(f32[16,128,256]{2,1,0:T(8,128)} %gather_fusion.10), channel_id=1, source_target_pairs={{0,254},{2,0},{4,2},{6,4},{8,6},{10,8},{12,10},{14,12},{16,14},{18... | collective-permute-start | bytes 6291464 | tf_op jit(solution)/shard_map/ppermute | solution.py:25
  949.9 32.0 %collective-permute-start.7 = (f32[16,128,256]{2,1,0:T(8,128)}, f32[16,128,256]{2,1,0:T(8,128)}, u32[]{:S(2)}, u32[]{:S(2)}) collective-permute-start(f32[16,128,256]{2,1,0:T(8,128)} %gather_fusion.11), channel_id=1, source_target_pairs={{0,2},{2,4},{4,6},{6,8},{8,10},{10,12},{12,14},{14,16},{16,18},{18... | collective-permute-start | bytes 6291464 | tf_op jit(solution)/shard_map/ppermute | solution.py:25
  978.5 3.5 copy-start.2
  978.5 3.5 copy-start.3
  987.1 1.3 copy-start.1
Sparse Core Ops, SparseCore 0:
  11.4 103.6 all-gather.1
where the time goes:
time: 1350 us
  blocking collectives  1040 us (77%)
  waiting for transfers between devices  136 us (10%)
  local copies, waits for them, and re-layouts  63.5 us (5%)
  matrix products  58.4 us (4%)
  starting transfers between devices  19.1 us (1%)
  other arithmetic  17.7 us (1%)
  between operations  14.2 us (1%)
    psum x2, blocking collectives, squares(): return lax.psum(jnp.sum(values * values, axis=0), 'vert')  692 us
    psum x1, blocking collectives, body(): curve = lax.psum(jnp.sum(direction * image, axis=0), 'vert')  347 us
    all_gather x1, waiting for transfers between devices, body(): lax.all_gather(queries, 'vert', axis=1, tiled=True)  100 us
    ppermute x4, waiting for transfers between devices, shifted(): return lax.ppermute(x, axis, [(i, (i + by) % peers) for i in range(peers)])  30 us
    dot_general x6, matrix products, transposed(): jnp.einsum('rba,rbq->raq', blocks_slot, rows3, precision=lax.Precision.HI...  27.8 us
  transfers between devices with their start and end apart: 9, of which 5 were waited for; matrix products, arithmetic and copies ran while one was open for 8% of the time, Pallas kernels for 0%

commit v1 on v0

--- a/solution.py
+++ b/solution.py
@@ -39,7 +39,9 @@
     here = lax.axis_index("vert")
     sims = lax.dot_general(
         descriptors,
-        lax.all_gather(queries, "vert", axis=1, tiled=True),
+        jnp.concatenate(
+            lax.all_to_all(jnp.stack([queries] * lax.axis_size("vert")), "vert", 0, 0), axis=1
+        ),
         (((1,), (1,)), ((), ())),
         preferred_element_type=jnp.float32,
     )

time: 1350 us -> 1290 us (0.956)
  waiting for transfers between devices: 136 us -> 61.7 us
  starting transfers between devices: 19.1 us -> 33.9 us
    all_gather x1 -> x0, waiting for transfers between devices: 100 us -> none  [body(): lax.all_gather(queries, 'vert', axis=1, tiled=True)]
    all_to_all x0 -> x1, waiting for transfers between devices: none -> 25.8 us  [body(): lax.all_to_all(jnp.stack([queries] * lax.axis_size('vert')), 'vert', 0, 0)]
    all_to_all x0 -> x1, starting transfers between devices: none -> 14.1 us  [body(): lax.all_to_all(jnp.stack([queries] * lax.axis_size('vert')), 'vert', 0, 0)]
where the time goes in v1:
time: 1290 us; the launch traced here: 1280 us
  blocking collectives  1040 us (81%)
  local copies, waits for them, and re-layouts  63.9 us (5%)
  waiting for transfers between devices  61.7 us (5%)
  matrix products  58.2 us (5%)
  starting transfers between devices  33.9 us (3%)
  other arithmetic  17.6 us (1%)
    psum x2, blocking collectives, squares(): return lax.psum(jnp.sum(values * values, axis=0), 'vert')  692 us
    psum x1, blocking collectives, body(): curve = lax.psum(jnp.sum(direction * image, axis=0), 'vert')  347 us
    ppermute x4, waiting for transfers between devices, shifted(): return lax.ppermute(x, axis, [(i, (i + by) % peers) for i in range(peers)])  31 us
    dot_general x6, matrix products, transposed(): jnp.einsum('rba,rbq->raq', blocks_slot, rows3, precision=lax.Precision.HI...  27.8 us
    all_to_all x1, waiting for transfers between devices, body(): lax.all_to_all(jnp.stack([queries] * lax.axis_size('vert')), 'vert', 0, 0)  25.8 us
  transfers between devices with their start and end apart: 9, of which 5 were waited for; matrix products, arithmetic and copies ran while one was open for 8% of the time, Pallas kernels for 0%

profile of v1, /device:TPU:0, one launch (start us, length us, event | category | flops | bytes accessed | tf_op | source)
XLA Modules:
  0.0 1276.0 jit_solution(10983612727115683058)
XLA Ops:
  2.4 14.1 %all-to-all-start = ((bf16[128,256,16]{1,2,0:T(8,128)(2,1)}), bf16[128,256,16]{1,2,0:T(8,128)(2,1)S(1)}, u32[]{:S(2)}, u32[]{:S(2)}) async-start(bf16[128,256,16]{1,2,0:T(8,128)(2,1)} %stack.2), calls=%async_computation | async-start | bytes 2097152 | tf_op jit(solution)/shard_map/all_to_all | solution.py:43
  21.8 25.8 %all-to-all-done = bf16[128,256,16]{1,2,0:T(8,128)(2,1)S(1)} async-done(((bf16[128,256,16]{1,2,0:T(8,128)(2,1)}), bf16[128,256,16]{1,2,0:T(8,128)(2,1)S(1)}, u32[]{:S(2)}, u32[]{:S(2)}) %all-to-all-start) | async-done | bytes 1048608 | tf_op jit(solution)/shard_map/all_to_all | solution.py:43
  47.6 5.8 fusion
  54.2 6.8 collective-permute-start.1
  61.0 4.3 convolution_bitcast_fusion.4
  71.8 4.3 convolution_bitcast_fusion.3
  85.8 4.3 convolution_bitcast_fusion.5
  98.6 4.1 fusion.17
  102.8 4.9 collective-permute-done
  107.7 3.6 gather_fusion
  111.3 3.7 gather_fusion.2
  118.0 29.8 %collective-permute-done.2 = f32[16,128,256]{2,1,0:T(8,128)} collective-permute-done((f32[16,128,256]{2,1,0:T(8,128)}, f32[16,128,256]{2,1,0:T(8,128)}, u32[]{:S(2)}, u32[]{:S(2)}) %collective-permute-start.2) | collective-permute-done | bytes 2097184 | tf_op jit(solution)/shard_map/ppermute | solution.py:25
  148.6 5.1 bitcast_add_fusion.1
  155.0 349.3 %all-reduce = (f32[256]{0:T(256)S(1)}, f32[256]{0:T(256)S(1)}) all-reduce(f32[256]{0:T(256)S(1)} %get-tuple-element.9, f32[256]{0:T(256)S(1)} %get-tuple-element.8), channel_id=1, replica_groups=mesh['vert'=128,'qcol'=2] {'vert'}, use_global_device_ids=true, to_apply=%region_1.2 | all-reduce | flops 512 | bytes 4096 | tf_op jit(solution)/shard_map/psum | solution.py:55
  506.4 343.0 %psum.30 = f32[256]{0:T(256)S(1)} all-reduce(f32[256]{0:T(256)S(1)} %multiply_reduce_fusion.1), channel_id=1, replica_groups=mesh['vert'=128,'qcol'=2] {'vert'}, use_global_device_ids=true, to_apply=%region_8.9 | all-reduce | flops 256 | bytes 2048 | tf_op jit(solution)/shard_map/psum | solution.py:55
  854.8 5.7 collective-permute-start.5
  860.5 5.0 convolution_bitcast_fusion.1
  871.9 4.9 convolution_bitcast_fusion
  889.3 5.0 convolution_bitcast_fusion.2
  897.2 3.6 gather_fusion.9
  900.8 4.1 fusion.14
  915.6 5.1 bitcast_add_fusion
  924.0 347.2 %psum.31 = f32[256]{0:T(256)S(1)} all-reduce(f32[256]{0:T(256)S(1)} %multiply_reduce_fusion), channel_id=1, replica_groups=mesh['vert'=128,'qcol'=2] {'vert'}, use_global_device_ids=true, to_apply=%region_10.11 | all-reduce | flops 256 | bytes 2048 | tf_op jit(solution)/shard_map/psum | solution.py:77
  1271.2 4.6 multiply_subtract_fusion
  (74 shorter events, 80.6 us)
Async XLA Ops:
  0.6 15.8 %copy-start.7 = (s32[128]{0:T(128)S(1)}, s32[128]{0:T(128)}, u32[]{:S(2)}) copy-start(s32[128]{0:T(128)} %param.9) | copy-start | bytes 1540
  0.6 16.5 %copy-start.6 = (s32[128,3,16]{0,2,1:T(8,128)S(1)}, s32[128,3,16]{0,2,1:T(8,128)}, u32[]{:S(2)}) copy-start(s32[128,3,16]{0,2,1:T(8,128)} %param.8) | copy-start | bytes 73732
  2.4 45.2 %all-to-all-start = ((bf16[128,256,16]{1,2,0:T(8,128)(2,1)}), bf16[128,256,16]{1,2,0:T(8,128)(2,1)S(1)}, u32[]{:S(2)}, u32[]{:S(2)}) async-start(bf16[128,256,16]{1,2,0:T(8,128)(2,1)} %stack.2), calls=%async_computation | async-start | bytes 2097152 | tf_op jit(solution)/shard_map/all_to_all | solution.py:43
  53.5 54.2 %collective-permute-start = (f32[2048,256]{1,0:T(8,128)S(1)}, f32[2048,256]{1,0:T(8,128)}, u32[]{:S(2)}, u32[]{:S(2)}) collective-permute-start(f32[2048,256]{1,0:T(8,128)S(1)} %fusion), channel_id=1, source_target_pairs={{0,2},{2,4},{4,6},{6,8},{8,10},{10,12},{12,14},{14,16},{16,18},{18... | collective-permute-start | bytes 6291464 | tf_op jit(solution)/shard_map/ppermute | solution.py:15
  54.2 57.1 %collective-permute-start.1 = (f32[2048,256]{1,0:T(8,128)S(1)}, f32[2048,256]{1,0:T(8,128)}, u32[]{:S(2)}, u32[]{:S(2)}) collective-permute-start(f32[2048,256]{1,0:T(8,128)S(1)} %fusion), channel_id=1, source_target_pairs={{2,0},{4,2},{6,4},{8,6},{10,8},{12,10},{14,12},{16,14},{18,16},{20... | collective-permute-start | bytes 6291464 | tf_op jit(solution)/shard_map/ppermute | solution.py:18
  71.8 76.0 %collective-permute-start.2 = (f32[16,128,256]{2,1,0:T(8,128)}, f32[16,128,256]{2,1,0:T(8,128)}, u32[]{:S(2)}, u32[]{:S(2)}) collective-permute-start(f32[16,128,256]{2,1,0:T(8,128)} %gather_fusion.4), channel_id=1, source_target_pairs={{0,254},{2,0},{4,2},{6,4},{8,6},{10,8},{12,10},{14,12},{16,14},{18... | collective-permute-start | bytes 6291464 | tf_op jit(solution)/shard_map/ppermute | solution.py:25
  82.6 66.0 %collective-permute-start.3 = (f32[16,128,256]{2,1,0:T(8,128)}, f32[16,128,256]{2,1,0:T(8,128)}, u32[]{:S(2)}, u32[]{:S(2)}) collective-permute-start(f32[16,128,256]{2,1,0:T(8,128)} %gather_fusion.5), channel_id=1, source_target_pairs={{0,2},{2,4},{4,6},{6,8},{8,10},{10,12},{12,14},{14,16},{16,18},{18... | collective-permute-start | bytes 6291464 | tf_op jit(solution)/shard_map/ppermute | solution.py:25
  115.0 33.6 %copy-start.4 = (f32[16,128,256]{2,1,0:T(8,128)S(1)}, f32[16,128,256]{2,1,0:T(8,128)}, u32[]{:S(2)}) copy-start(f32[16,128,256]{2,1,0:T(8,128)} %gather_fusion.3) | copy-start | bytes 6291460
  115.0 33.6 %copy-start.5 = (f32[16,256,128]{1,2,0:T(8,128)S(1)}, f32[16,256,128]{1,2,0:T(8,128)}, u32[]{:S(2)}) copy-start(f32[16,256,128]{1,2,0:T(8,128)} %fusion.17) | copy-start | bytes 6291460
  153.7 1.4 copy-start
  852.9 52.1 %collective-permute-start.4 = (f32[2048,256]{1,0:T(8,128)}, f32[2048,256]{1,0:T(8,128)}, u32[]{:S(2)}, u32[]{:S(2)}) collective-permute-start(f32[2048,256]{1,0:T(8,128)} %multiply_add_fusion.1), channel_id=1, source_target_pairs={{0,2},{2,4},{4,6},{6,8},{8,10},{10,12},{12,14},{14,16},{16,18},{18... | collective-permute-start | bytes 6291464 | tf_op jit(solution)/shard_map/ppermute | solution.py:15
  854.8 53.7 %collective-permute-start.5 = (f32[2048,256]{1,0:T(8,128)}, f32[2048,256]{1,0:T(8,128)}, u32[]{:S(2)}, u32[]{:S(2)}) collective-permute-start(f32[2048,256]{1,0:T(8,128)} %multiply_add_fusion.1), channel_id=1, source_target_pairs={{2,0},{4,2},{6,4},{8,6},{10,8},{12,10},{14,12},{16,14},{18,16},{20... | collective-permute-start | bytes 6291464 | tf_op jit(solution)/shard_map/ppermute | solution.py:18
  871.9 43.2 %collective-permute-start.6 = (f32[16,128,256]{2,1,0:T(8,128)}, f32[16,128,256]{2,1,0:T(8,128)}, u32[]{:S(2)}, u32[]{:S(2)}) collective-permute-start(f32[16,128,256]{2,1,0:T(8,128)} %gather_fusion.10), channel_id=1, source_target_pairs={{0,254},{2,0},{4,2},{6,4},{8,6},{10,8},{12,10},{14,12},{16,14},{18... | collective-permute-start | bytes 6291464 | tf_op jit(solution)/shard_map/ppermute | solution.py:25
  883.4 32.1 %collective-permute-start.7 = (f32[16,128,256]{2,1,0:T(8,128)}, f32[16,128,256]{2,1,0:T(8,128)}, u32[]{:S(2)}, u32[]{:S(2)}) collective-permute-start(f32[16,128,256]{2,1,0:T(8,128)} %gather_fusion.11), channel_id=1, source_target_pairs={{0,2},{2,4},{4,6},{6,8},{8,10},{10,12},{12,14},{14,16},{16,18},{18... | collective-permute-start | bytes 6291464 | tf_op jit(solution)/shard_map/ppermute | solution.py:25
  912.1 3.5 copy-start.2
  912.1 3.5 copy-start.3
  920.7 1.3 copy-start.1
